TPU v7x, 32 devices: a whole 2x2x4 slice. The times are simulated.
32 devices in a mesh: ax: 2 (over x), az: 4 (over z), rad: 4 (over y, core).
Axes of the slice: x: 2, y: 2, z: 4, core: 2. Of those that a mesh axis runs over, the one named last changes fastest.
Arguments:
- velocity: float32 [512, 64, 512], P('rad', 'az', 'ax'), may hold values from -4 to 4
- radial_courant: bfloat16 [512, 64, 512], P('rad', 'az', 'ax'), may hold values from -0.5 to 0.5
- axial_courant: bfloat16 [512, 64, 512], P('rad', 'az', 'ax'), may hold values from -0.5 to 0.5
- radial_diffusion: float32 [512], P('rad'), may hold values from 2048 to 8192
Outputs:
- advanced: float32 [512, 64, 512], P('rad', 'az', 'ax')
All inputs are finite; a program needn't handle non-finite values.
Results may differ from a plain program's by a relative error of at most 0.0009.
Values sent between devices are 32-bit elements; how exact they have to be, the bound alone decides.
A program may use at most 64 MiB of HBM per device.

v0:
```python
from functools import partial

import jax
import jax.numpy as jnp
from jax import lax
from jax.sharding import PartitionSpec as P

NR = 512
STEPS = 6


theta_rate = 0.25
axial_mixing = 0.25
azimuth_mixing = 0.25


def padded(block, sides, width, periodic):
    for axis, dim in sides:
        count = lax.axis_size(axis)
        forward = [(i, i + 1) for i in range(count - 1)]
        if periodic:
            forward.append((count - 1, 0))
        backward = [(target, source) for source, target in forward]
        low = lax.ppermute(
            lax.slice_in_dim(block, block.shape[dim] - width, None, axis=dim), axis, forward
        )
        high = lax.ppermute(lax.slice_in_dim(block, 0, width, axis=dim), axis, backward)
        block = jnp.concatenate([low, block, high], axis=dim)
    return block


def radial_terms(radial_diffusion, position):
    spacing = 1.0 / (NR + 1)
    radius = 1.0 + (position + 1.0) * spacing
    inward = radial_diffusion * (radius - 0.5 * spacing) / radius
    outward = radial_diffusion * (radius + 0.5 * spacing) / radius
    curvature = radial_diffusion * spacing * spacing / (radius * radius)
    return (radius, inward, outward, curvature)


def right_side(
    state_field,
    radial_lower,
    radial_upper,
    axial_minus_two,
    axial_minus_one,
    axial_plus_one,
    axial_plus_two,
    azimuth_minus_two,
    azimuth_minus_one,
    azimuth_plus_one,
    azimuth_plus_two,
    radial_courant,
    axial_courant,
    radius,
    inward,
    outward,
    curvature,
):
    radius_col = radius[:, None, None]
    spread = (
        outward[:, None, None] * (radial_upper - state_field)
        - inward[:, None, None] * (state_field - radial_lower)
        - curvature[:, None, None] * state_field
    )
    radial_slope = 0.5 * (radial_upper - radial_lower)
    axial_slope = (
        8.0 * (axial_plus_one - axial_minus_one) - (axial_plus_two - axial_minus_two)
    ) / 12.0
    axial_curve = (
        16.0 * (axial_plus_one + axial_minus_one)
        - (axial_plus_two + axial_minus_two)
        - 30.0 * state_field
    ) / 12.0
    azimuth_slope = (
        8.0 * (azimuth_plus_one - azimuth_minus_one) - (azimuth_plus_two - azimuth_minus_two)
    ) / 12.0
    azimuth_curve = (
        16.0 * (azimuth_plus_one + azimuth_minus_one)
        - (azimuth_plus_two + azimuth_minus_two)
        - 30.0 * state_field
    ) / 12.0
    transport = (
        radial_courant * radial_slope
        + axial_courant * axial_slope
        + theta_rate * state_field * azimuth_slope / radius_col
    )
    mixing = axial_mixing * axial_curve + azimuth_mixing * azimuth_curve / (radius_col * radius_col)
    return state_field + spread - transport + mixing


def neighbours(state_field):
    slab_rows, theta_cells, axial_cells = state_field.shape
    radial_ext = padded(state_field, (("rad", 0),), 1, False)
    radial_lower = radial_ext[:-2]
    radial_upper = radial_ext[2:]
    azimuth_ext = padded(state_field, (("az", 1),), 2, True)
    axial_ext = padded(state_field, (("ax", 2),), 2, False)
    return (
        radial_lower,
        radial_upper,
        axial_ext[:, :, 0:axial_cells],
        axial_ext[:, :, 1 : axial_cells + 1],
        axial_ext[:, :, 3 : axial_cells + 3],
        axial_ext[:, :, 4 : axial_cells + 4],
        azimuth_ext[:, 0:theta_cells],
        azimuth_ext[:, 1 : theta_cells + 1],
        azimuth_ext[:, 3 : theta_cells + 3],
        azimuth_ext[:, 4 : theta_cells + 4],
    )


def join_slabs(earlier, later_seg):
    head_left, tail_left, tips_left = earlier
    head_right, tail_right, tips_right = later_seg
    divisor = 1.0 - tips_left[3] * tips_right[0]
    mid_value = (tail_left - tips_left[3] * head_right) / divisor
    mid_left = tips_left[2] / divisor
    mid_right = -tips_left[3] * tips_right[1] / divisor
    next_value = head_right - tips_right[0] * mid_value
    next_left = -tips_right[0] * mid_left
    next_right = tips_right[1] - tips_right[0] * mid_right
    new_head = head_left - tips_left[1] * next_value
    new_tail = tail_right - tips_right[2] * mid_value
    new_tips = jnp.stack(
        [
            tips_left[0] - tips_left[1] * next_left,
            -tips_left[1] * next_right,
            -tips_right[2] * mid_left,
            tips_right[3] - tips_right[2] * mid_right,
        ]
    )
    return (new_head, new_tail, new_tips)


def choose(keep_new, fresh_value, stale_value):
    return jnp.where(keep_new, fresh_value, stale_value)


def settle(prefix, own_slab, suffix):
    combined = join_slabs(own_slab, suffix)
    pre_first, pre_last, pre_tips = prefix
    own_first, own_last, own_tips = own_slab
    suf_first, suf_last, suf_tips = suffix
    lower_value = (pre_last - pre_tips[3] * combined[0]) / (1.0 - pre_tips[3] * combined[2][0])
    upper_value = (suf_first - suf_tips[0] * (own_last - own_tips[2] * lower_value)) / (
        1.0 - suf_tips[0] * own_tips[3]
    )
    return (lower_value, upper_value)


def interface(first_row, last_row, spike_tips, every_tips):
    own_slab = (first_row, last_row, spike_tips)
    identity = (
        jnp.zeros_like(first_row),
        jnp.zeros_like(last_row),
        jnp.array([0.0, -1.0, -1.0, 0.0], jnp.float32),
    )
    every_first, every_last = (
        lax.all_gather(first_row[None], "rad", axis=0, tiled=True),
        lax.all_gather(last_row[None], "rad", axis=0, tiled=True),
    )
    position = lax.axis_index("rad")
    slab_count = lax.axis_size("rad")
    prefix = identity
    for index_k in range(slab_count):
        member = (every_first[index_k], every_last[index_k], every_tips[index_k])
        joined = join_slabs(prefix, member)
        prefix = jax.tree.map(partial(choose, index_k < position), joined, prefix)
    suffix = identity
    for index_k in range(slab_count - 1, -1, -1):
        member = (every_first[index_k], every_last[index_k], every_tips[index_k])
        joined = join_slabs(member, suffix)
        suffix = jax.tree.map(partial(choose, index_k > position), joined, suffix)
    return settle(prefix, own_slab, suffix)


def local(velocity, radial_courant, axial_courant, radial_diffusion):
    slab_rows = velocity.shape[0]
    start_row = (lax.axis_index("rad") * slab_rows).astype(jnp.float32)
    position = start_row + jnp.arange(slab_rows).astype(jnp.float32)
    radius, inward, outward, curvature = radial_terms(radial_diffusion, position)
    zero_one = jnp.zeros((1,), jnp.float32)
    lower_diag = jnp.concatenate([zero_one, -inward[1:]])
    upper_diag = jnp.concatenate([-outward[:-1], zero_one])
    main_diag = 1.0 + inward + outward + curvature
    inverse = lax.linalg.tridiagonal_solve(
        lower_diag, main_diag, upper_diag, jnp.eye(slab_rows, dtype=jnp.float32)
    )
    left_spike = -inward[0] * inverse[:, 0]
    right_spike = -outward[-1] * inverse[:, -1]
    spike_tips = jnp.stack([left_spike[0], right_spike[0], left_spike[-1], right_spike[-1]])
    every_tips = lax.all_gather(spike_tips[None], "rad", axis=0, tiled=True)
    state_field = velocity
    for turn_index in range(STEPS):
        right_hand = right_side(
            state_field,
            *neighbours(state_field),
            radial_courant,
            axial_courant,
            radius,
            inward,
            outward,
            curvature
        )
        flat_rhs = right_hand.reshape(slab_rows, -1)
        slab_solution = jnp.dot(
            inverse, flat_rhs, precision=lax.Precision.HIGHEST, preferred_element_type=jnp.float32
        )
        lower_value, upper_value = interface(
            slab_solution[0], slab_solution[-1], spike_tips, every_tips
        )
        solved = (
            slab_solution
            - left_spike[:, None] * lower_value[None, :]
            - right_spike[:, None] * upper_value[None, :]
        )
        state_field = solved.reshape(state_field.shape)
    return state_field


def solution(mesh):
    return jax.shard_map(
        local,
        mesh=mesh,
        in_specs=(P("rad", "az", "ax"), P("rad", "az", "ax"), P("rad", "az", "ax"), P("rad")),
        out_specs=P("rad", "az", "ax"),
        check_vma=False,
    )
```

profile of v0, /device:TPU:0, one launch (start us, length us, event | category | flops | bytes accessed | tf_op | source)
XLA Modules:
  0.0 981.2 jit_solution(10601417094346248530)
XLA Ops:
  16.5 5.7 collective-permute-start.3
  26.0 253.8 %while.32 = (s32[]{:T(128)}, f32[]{:T(128)}, f32[128]{0:T(128)S(1)}, f32[3,32]{1,0:T(4,128)S(1)}, f32[3,32,128]{2,1,0:T(8,128)S(1)}, /*index=5*/f32[3,32]{1,0:T(...) while((s32[]{:T(128)}, f32[]{:T(128)}, ...), condition=%wide.region_1.2_spmd, body=%wide.region_0.1_spmd.sunk | while | flops 12417 | bytes 104185 | solution.py:187
  90.2 20.2 %fusion.565 = (f32[128]{0:T(128)S(1)}, f32[128]{0:T(128)S(1)}, f32[128]{0:T(128)S(1)}, f32[128]{0:T(128)S(1)}, f32[128]{0:T(128)S(1)}, /*index=5*/f32[128]{0:T(1...) fusion(f32[3,32,128]{2,1,0:T(8,128)S(1)} %get-tuple-element.125, ...), kind=kLoop, calls=%fused_computation.41.clone.1 | loop fusion | flops 12288 | bytes 33664 | tf_op jit(solution)/shard_map/while/body/eval_jaxpr/div | solution.py:187
  174.8 20.2 %fusion.565 = (f32[128]{0:T(128)S(1)}, f32[128]{0:T(128)S(1)}, f32[128]{0:T(128)S(1)}, f32[128]{0:T(128)S(1)}, f32[128]{0:T(128)S(1)}, /*index=5*/f32[128]{0:T(1...) fusion(f32[3,32,128]{2,1,0:T(8,128)S(1)} %get-tuple-element.125, ...), kind=kLoop, calls=%fused_computation.41.clone.1 | loop fusion | flops 12288 | bytes 33664 | tf_op jit(solution)/shard_map/while/body/eval_jaxpr/div | solution.py:187
  259.4 20.2 %fusion.565 = (f32[128]{0:T(128)S(1)}, f32[128]{0:T(128)S(1)}, f32[128]{0:T(128)S(1)}, f32[128]{0:T(128)S(1)}, f32[128]{0:T(128)S(1)}, /*index=5*/f32[128]{0:T(1...) fusion(f32[3,32,128]{2,1,0:T(8,128)S(1)} %get-tuple-element.125, ...), kind=kLoop, calls=%fused_computation.41.clone.1 | loop fusion | flops 12288 | bytes 33664 | tf_op jit(solution)/shard_map/while/body/eval_jaxpr/div | solution.py:187
  342.2 19.2 %fusion.330 = (f32[128]{0:T(128)S(1)}, f32[128]{0:T(128)S(1)}, f32[128]{0:T(128)S(1)}, f32[128]{0:T(128)S(1)}, f32[128]{0:T(128)S(1)}, /*index=5*/f32[128]{0:T(1...) fusion(f32[128,128]{1,0:T(8,128)S(1)} %fusion.256, ...), kind=kLoop, calls=%fused_computation.662 | loop fusion | flops 11904 | bytes 32504 | tf_op jit(solution)/shard_map/eval_jaxpr/div | solution.py:187
  361.8 65.2 %while.33 = (s32[]{:T(128)}, f32[128]{0:T(128)S(1)}, f32[3,32,128]{2,1,0:T(8,128)S(1)}, f32[3,32,128]{2,1,0:T(8,128)S(1)}, f32[3,32]{1,0:T(4,128)S(1)}, /*index=...) while((s32[]{:T(128)}, f32[128]{0:T(128)S(1)}, ...), condition=%wide.region_3.4_spmd, body=%wide.region_2.3_spmd.sunk | while | flops 8226 | bytes 101341 | solution.py:187
  363.3 20.2 %fusion.568 = (f32[128]{0:T(128)S(1)}, f32[128]{0:T(128)S(1)}, f32[128]{0:T(128)S(1)}, f32[128]{0:T(128)S(1)}, f32[128]{0:T(128)S(1)}, /*index=5*/f32[128]{0:T(1...) fusion(f32[3,32,128]{2,1,0:T(8,128)S(1)} %get-tuple-element.136, ...), kind=kLoop, calls=%fused_computation.169.clone.1 | loop fusion | flops 8192 | bytes 33536 | tf_op jit(solution)/shard_map/while/body/eval_jaxpr/sub | solution.py:187
  385.0 20.2 %fusion.568 = (f32[128]{0:T(128)S(1)}, f32[128]{0:T(128)S(1)}, f32[128]{0:T(128)S(1)}, f32[128]{0:T(128)S(1)}, f32[128]{0:T(128)S(1)}, /*index=5*/f32[128]{0:T(1...) fusion(f32[3,32,128]{2,1,0:T(8,128)S(1)} %get-tuple-element.136, ...), kind=kLoop, calls=%fused_computation.169.clone.1 | loop fusion | flops 8192 | bytes 33536 | tf_op jit(solution)/shard_map/while/body/eval_jaxpr/sub | solution.py:187
  406.8 20.2 %fusion.568 = (f32[128]{0:T(128)S(1)}, f32[128]{0:T(128)S(1)}, f32[128]{0:T(128)S(1)}, f32[128]{0:T(128)S(1)}, f32[128]{0:T(128)S(1)}, /*index=5*/f32[128]{0:T(1...) fusion(f32[3,32,128]{2,1,0:T(8,128)S(1)} %get-tuple-element.136, ...), kind=kLoop, calls=%fused_computation.169.clone.1 | loop fusion | flops 8192 | bytes 33536 | tf_op jit(solution)/shard_map/while/body/eval_jaxpr/sub | solution.py:187
  494.3 6.0 all-reduce
  580.0 14.9 %fusion.181 = f32[128,16,256]{2,1,0:T(8,128)S(1)} fusion(bf16[128,16,256]{2,1,0:T(8,128)(2,1)S(1)} %copy-done, bf16[128,16,256]{2,1,0:T(8,128)(2,1)S(1)} %copy-done.1, f32[128,16,256]{2,1,0:T(8,128)} %param.14, f32[1,16,256]{2,1,0:T(8,128)} %collective-permute-done.1, f32[1,16,256]{2,1,0:T(8,128)S(1)} %collective-permute-done, ...), kind=kLoop, calls=%fused_computation.299 | loop fusion | flops 28311552 | bytes 10816000 | tf_op jit(solution)/shard_map/add | solution.py:89
  598.6 5.9 all-gather.2
  609.7 13.5 %subtract_divide_fusion.5 = (f32[1,4096]{1,0:T(1,128)S(1)}, f32[1,4096]{1,0:T(1,128)S(1)}) fusion(f32[]{:T(128)} %bitcast.672, f32[]{:T(128)S(6)} %sub.2725, f32[]{:T(128)S(1)} %bitcast.2392, f32[128,4096]{1,0:T(8,128)S(1)} %fusion.531, f32[]{:T(128)S(6)} %sub.2730, f32[]{:T(128)} %bitcast.670, f32[]{:T(128)} %bitcast.640, f32[]{:T(128)} %bitcast.639, ...), kind=kLoop, calls=%fused_computation.547 | loop fusion | flops 286720 | bytes 196748 | tf_op jit(solution)/shard_map/div | solution.py:146
  654.2 9.4 fusion.185
  667.3 7.8 all-gather.4
  675.1 5.5 all-gather.3
  680.6 13.5 %subtract_divide_fusion.4 = (f32[1,4096]{1,0:T(1,128)S(1)}, f32[1,4096]{1,0:T(1,128)S(1)}) fusion(f32[]{:T(128)} %bitcast.672, f32[]{:T(128)S(6)} %sub.2725, f32[]{:T(128)S(1)} %bitcast.2393, f32[128,4096]{1,0:T(8,128)S(1)} %fusion.532, f32[]{:T(128)S(6)} %sub.2730, f32[]{:T(128)} %bitcast.670, f32[]{:T(128)} %bitcast.640, f32[]{:T(128)} %bitcast.639, ...), kind=kLoop, calls=%fused_computation.546 | loop fusion | flops 286720 | bytes 196748 | tf_op jit(solution)/shard_map/div | solution.py:146
  725.3 9.4 fusion.189
  738.4 7.9 all-gather.6
  746.3 5.5 all-gather.5
  751.8 13.5 %subtract_divide_fusion.3 = (f32[1,4096]{1,0:T(1,128)S(1)}, f32[1,4096]{1,0:T(1,128)S(1)}) fusion(f32[]{:T(128)} %bitcast.672, f32[]{:T(128)S(6)} %sub.2725, f32[]{:T(128)S(1)} %bitcast.2394, f32[128,4096]{1,0:T(8,128)S(1)} %fusion.533, f32[]{:T(128)S(6)} %sub.2730, f32[]{:T(128)} %bitcast.670, f32[]{:T(128)} %bitcast.640, f32[]{:T(128)} %bitcast.639, ...), kind=kLoop, calls=%fused_computation.545 | loop fusion | flops 286720 | bytes 196748 | tf_op jit(solution)/shard_map/div | solution.py:146
  796.3 9.4 fusion.193
  809.3 7.9 all-gather.8
  817.3 5.5 all-gather.7
  822.8 13.5 %subtract_divide_fusion.2 = (f32[1,4096]{1,0:T(1,128)S(1)}, f32[1,4096]{1,0:T(1,128)S(1)}) fusion(f32[]{:T(128)} %bitcast.672, f32[]{:T(128)S(6)} %sub.2725, f32[]{:T(128)S(1)} %bitcast.2395, f32[128,4096]{1,0:T(8,128)S(1)} %fusion.534, f32[]{:T(128)S(6)} %sub.2730, f32[]{:T(128)} %bitcast.670, f32[]{:T(128)} %bitcast.640, f32[]{:T(128)} %bitcast.639, ...), kind=kLoop, calls=%fused_computation.544 | loop fusion | flops 286720 | bytes 196748 | tf_op jit(solution)/shard_map/div | solution.py:146
  867.3 9.4 fusion.197
  880.4 7.9 all-gather.10
  893.8 13.5 %subtract_divide_fusion.1 = (f32[1,4096]{1,0:T(1,128)S(1)}, f32[1,4096]{1,0:T(1,128)S(1)}) fusion(f32[]{:T(128)} %bitcast.672, f32[]{:T(128)S(6)} %sub.2725, f32[]{:T(128)S(1)} %bitcast.2396, f32[128,4096]{1,0:T(8,128)S(1)} %fusion.535, f32[]{:T(128)S(6)} %sub.2730, f32[]{:T(128)} %bitcast.670, f32[]{:T(128)} %bitcast.640, f32[]{:T(128)} %bitcast.639, ...), kind=kLoop, calls=%fused_computation.543 | loop fusion | flops 286720 | bytes 196748 | tf_op jit(solution)/shard_map/div | solution.py:146
  938.4 9.4 fusion.201
  951.4 7.9 all-gather.12
  964.9 13.5 %subtract_divide_fusion = (f32[1,4096]{1,0:T(1,128)S(1)}, f32[1,4096]{1,0:T(1,128)S(1)}) fusion(f32[]{:T(128)} %bitcast.672, f32[]{:T(128)S(6)} %sub.2725, f32[]{:T(128)S(1)} %bitcast.2397, f32[128,4096]{1,0:T(8,128)S(1)} %fusion.536, f32[]{:T(128)S(6)} %sub.2730, f32[]{:T(128)} %bitcast.670, f32[]{:T(128)} %bitcast.640, f32[]{:T(128)} %bitcast.639, ...), kind=kLoop, calls=%fused_computation.542 | loop fusion | flops 286720 | bytes 196748 | tf_op jit(solution)/shard_map/div | solution.py:146
  (349 shorter events, 318.7 us)
Async XLA Ops:
  1.3 578.7 %collective-permute-start.1 = (f32[1,16,256]{2,1,0:T(8,128)}, f32[1,16,256]{2,1,0:T(8,128)}, u32[]{:S(2)}, u32[]{:S(2)}) collective-permute-start(f32[1,16,256]{2,1,0:T(8,128)} %get-tuple-element.511), channel_id=1, source_target_pairs={{0,1},{1,2},{2,3},{4,5},{5,6},{6,7},{8,9},{9,10},{10,11},{12,13},{... | collective-permute-start | bytes 49160 | tf_op jit(solution)/shard_map/ppermute | solution.py:24
  6.8 573.2 %collective-permute-start.5 = (f32[128,2,256]{2,1,0:T(2,128)}, f32[128,2,256]{2,1,0:T(2,128)S(1)}, u32[]{:S(2)}, u32[]{:S(2)}) collective-permute-start(f32[128,2,256]{2,1,0:T(2,128)} %get-tuple-element.509), channel_id=1, source_target_pairs={{0,4},{4,8},{8,12},{12,0},{1,5},{5,9},{9,13},{13,1},{2,6},{6,10},{... | collective-permute-start | bytes 786440 | tf_op jit(solution)/shard_map/ppermute | solution.py:24
  9.2 569.0 %collective-permute-start.4 = (f32[128,2,256]{2,1,0:T(2,128)}, f32[128,2,256]{2,1,0:T(2,128)}, u32[]{:S(2)}, u32[]{:S(2)}) collective-permute-start(f32[128,2,256]{2,1,0:T(2,128)} %get-tuple-element.508), channel_id=1, source_target_pairs={{4,0},{8,4},{12,8},{0,12},{5,1},{9,5},{13,9},{1,13},{6,2},{10,6},{... | collective-permute-start | bytes 786440 | tf_op jit(solution)/shard_map/ppermute | solution.py:27
  14.2 559.2 %collective-permute-start.2 = (f32[128,16,2]{0,1,2:T(8,128)}, f32[128,16,2]{0,1,2:T(8,128)}, u32[]{:S(2)}, u32[]{:S(2)}) collective-permute-start(f32[128,16,2]{0,1,2:T(8,128)} %copy.101), channel_id=1, source_target_pairs={{16,0},{17,1},{18,2},{19,3},{20,4},{21,5},{22,6},{23,7},{24,8},{25... | collective-permute-start | bytes 49160 | tf_op jit(solution)/shard_map/ppermute | solution.py:27
  16.5 559.6 %collective-permute-start.3 = (f32[128,16,2]{0,1,2:T(8,128)}, f32[128,16,2]{0,1,2:T(8,128)}, u32[]{:S(2)}, u32[]{:S(2)}) collective-permute-start(f32[128,16,2]{0,1,2:T(8,128)} %copy.102), channel_id=1, source_target_pairs={{0,16},{1,17},{2,18},{3,19},{4,20},{5,21},{6,22},{7,23},{8,24},{9,... | collective-permute-start | bytes 49160 | tf_op jit(solution)/shard_map/ppermute | solution.py:24
  627.6 26.7 %collective-permute-start.11 = (f32[128,2,256]{2,1,0:T(2,128)}, f32[128,2,256]{2,1,0:T(2,128)S(1)}, u32[]{:S(2)}, u32[]{:S(2)}) collective-permute-start(f32[128,2,256]{2,1,0:T(2,128)} %get-tuple-element.503), channel_id=1, source_target_pairs={{0,4},{4,8},{8,12},{12,0},{1,5},{5,9},{9,13},{13,1},{2,6},{6,10},{... | collective-permute-start | bytes 786440 | tf_op jit(solution)/shard_map/ppermute | solution.py:24
  627.6 24.9 %collective-permute-start.10 = (f32[128,2,256]{2,1,0:T(2,128)}, f32[128,2,256]{2,1,0:T(2,128)}, u32[]{:S(2)}, u32[]{:S(2)}) collective-permute-start(f32[128,2,256]{2,1,0:T(2,128)} %get-tuple-element.502), channel_id=1, source_target_pairs={{4,0},{8,4},{12,8},{0,12},{5,1},{9,5},{13,9},{1,13},{6,2},{10,6},{... | collective-permute-start | bytes 786440 | tf_op jit(solution)/shard_map/ppermute | solution.py:27
  635.2 12.2 %collective-permute-start.8 = (f32[128,16,2]{0,1,2:T(8,128)}, f32[128,16,2]{0,1,2:T(8,128)S(1)}, u32[]{:S(2)}, u32[]{:S(2)}) collective-permute-start(f32[128,16,2]{0,1,2:T(8,128)} %copy.103), channel_id=1, source_target_pairs={{16,0},{17,1},{18,2},{19,3},{20,4},{21,5},{22,6},{23,7},{24,8},{25... | collective-permute-start | bytes 49160 | tf_op jit(solution)/shard_map/ppermute | solution.py:27
  638.7 11.6 %collective-permute-start.9 = (f32[128,16,2]{0,1,2:T(8,128)}, f32[128,16,2]{0,1,2:T(8,128)}, u32[]{:S(2)}, u32[]{:S(2)}) collective-permute-start(f32[128,16,2]{0,1,2:T(8,128)} %copy.104), channel_id=1, source_target_pairs={{0,16},{1,17},{2,18},{3,19},{4,20},{5,21},{6,22},{7,23},{8,24},{9,... | collective-permute-start | bytes 49160 | tf_op jit(solution)/shard_map/ppermute | solution.py:24
  645.5 8.8 collective-permute-start.7
  698.4 26.8 %collective-permute-start.17 = (f32[128,2,256]{2,1,0:T(2,128)}, f32[128,2,256]{2,1,0:T(2,128)S(1)}, u32[]{:S(2)}, u32[]{:S(2)}) collective-permute-start(f32[128,2,256]{2,1,0:T(2,128)} %get-tuple-element.497), channel_id=1, source_target_pairs={{0,4},{4,8},{8,12},{12,0},{1,5},{5,9},{9,13},{13,1},{2,6},{6,10},{... | collective-permute-start | bytes 786440 | tf_op jit(solution)/shard_map/ppermute | solution.py:24
  698.4 25.0 %collective-permute-start.16 = (f32[128,2,256]{2,1,0:T(2,128)}, f32[128,2,256]{2,1,0:T(2,128)}, u32[]{:S(2)}, u32[]{:S(2)}) collective-permute-start(f32[128,2,256]{2,1,0:T(2,128)} %get-tuple-element.496), channel_id=1, source_target_pairs={{4,0},{8,4},{12,8},{0,12},{5,1},{9,5},{13,9},{1,13},{6,2},{10,6},{... | collective-permute-start | bytes 786440 | tf_op jit(solution)/shard_map/ppermute | solution.py:27
  706.0 12.2 %collective-permute-start.14 = (f32[128,16,2]{0,1,2:T(8,128)}, f32[128,16,2]{0,1,2:T(8,128)S(1)}, u32[]{:S(2)}, u32[]{:S(2)}) collective-permute-start(f32[128,16,2]{0,1,2:T(8,128)} %copy.105), channel_id=1, source_target_pairs={{16,0},{17,1},{18,2},{19,3},{20,4},{21,5},{22,6},{23,7},{24,8},{25... | collective-permute-start | bytes 49160 | tf_op jit(solution)/shard_map/ppermute | solution.py:27
  709.5 11.8 %collective-permute-start.15 = (f32[128,16,2]{0,1,2:T(8,128)}, f32[128,16,2]{0,1,2:T(8,128)}, u32[]{:S(2)}, u32[]{:S(2)}) collective-permute-start(f32[128,16,2]{0,1,2:T(8,128)} %copy.106), channel_id=1, source_target_pairs={{0,16},{1,17},{2,18},{3,19},{4,20},{5,21},{6,22},{7,23},{8,24},{9,... | collective-permute-start | bytes 49160 | tf_op jit(solution)/shard_map/ppermute | solution.py:24
  716.3 9.0 collective-permute-start.13
  718.2 7.1 collective-permute-start.12
  769.7 26.6 %collective-permute-start.23 = (f32[128,2,256]{2,1,0:T(2,128)}, f32[128,2,256]{2,1,0:T(2,128)S(1)}, u32[]{:S(2)}, u32[]{:S(2)}) collective-permute-start(f32[128,2,256]{2,1,0:T(2,128)} %get-tuple-element.491), channel_id=1, source_target_pairs={{0,4},{4,8},{8,12},{12,0},{1,5},{5,9},{9,13},{13,1},{2,6},{6,10},{... | collective-permute-start | bytes 786440 | tf_op jit(solution)/shard_map/ppermute | solution.py:24
  769.7 24.8 %collective-permute-start.22 = (f32[128,2,256]{2,1,0:T(2,128)}, f32[128,2,256]{2,1,0:T(2,128)}, u32[]{:S(2)}, u32[]{:S(2)}) collective-permute-start(f32[128,2,256]{2,1,0:T(2,128)} %get-tuple-element.490), channel_id=1, source_target_pairs={{4,0},{8,4},{12,8},{0,12},{5,1},{9,5},{13,9},{1,13},{6,2},{10,6},{... | collective-permute-start | bytes 786440 | tf_op jit(solution)/shard_map/ppermute | solution.py:27
  777.2 12.2 %collective-permute-start.20 = (f32[128,16,2]{0,1,2:T(8,128)}, f32[128,16,2]{0,1,2:T(8,128)S(1)}, u32[]{:S(2)}, u32[]{:S(2)}) collective-permute-start(f32[128,16,2]{0,1,2:T(8,128)} %copy.107), channel_id=1, source_target_pairs={{16,0},{17,1},{18,2},{19,3},{20,4},{21,5},{22,6},{23,7},{24,8},{25... | collective-permute-start | bytes 49160 | tf_op jit(solution)/shard_map/ppermute | solution.py:27
  780.7 11.6 %collective-permute-start.21 = (f32[128,16,2]{0,1,2:T(8,128)}, f32[128,16,2]{0,1,2:T(8,128)}, u32[]{:S(2)}, u32[]{:S(2)}) collective-permute-start(f32[128,16,2]{0,1,2:T(8,128)} %copy.108), channel_id=1, source_target_pairs={{0,16},{1,17},{2,18},{3,19},{4,20},{5,21},{6,22},{7,23},{8,24},{9,... | collective-permute-start | bytes 49160 | tf_op jit(solution)/shard_map/ppermute | solution.py:24
  787.5 8.7 collective-permute-start.19
  840.6 26.7 %collective-permute-start.29 = (f32[128,2,256]{2,1,0:T(2,128)}, f32[128,2,256]{2,1,0:T(2,128)S(1)}, u32[]{:S(2)}, u32[]{:S(2)}) collective-permute-start(f32[128,2,256]{2,1,0:T(2,128)} %get-tuple-element.485), channel_id=1, source_target_pairs={{0,4},{4,8},{8,12},{12,0},{1,5},{5,9},{9,13},{13,1},{2,6},{6,10},{... | collective-permute-start | bytes 786440 | tf_op jit(solution)/shard_map/ppermute | solution.py:24
  840.6 24.9 %collective-permute-start.28 = (f32[128,2,256]{2,1,0:T(2,128)}, f32[128,2,256]{2,1,0:T(2,128)}, u32[]{:S(2)}, u32[]{:S(2)}) collective-permute-start(f32[128,2,256]{2,1,0:T(2,128)} %get-tuple-element.484), channel_id=1, source_target_pairs={{4,0},{8,4},{12,8},{0,12},{5,1},{9,5},{13,9},{1,13},{6,2},{10,6},{... | collective-permute-start | bytes 786440 | tf_op jit(solution)/shard_map/ppermute | solution.py:27
  848.2 12.2 %collective-permute-start.26 = (f32[128,16,2]{0,1,2:T(8,128)}, f32[128,16,2]{0,1,2:T(8,128)S(1)}, u32[]{:S(2)}, u32[]{:S(2)}) collective-permute-start(f32[128,16,2]{0,1,2:T(8,128)} %copy.109), channel_id=1, source_target_pairs={{16,0},{17,1},{18,2},{19,3},{20,4},{21,5},{22,6},{23,7},{24,8},{25... | collective-permute-start | bytes 49160 | tf_op jit(solution)/shard_map/ppermute | solution.py:27
  851.7 11.6 %collective-permute-start.27 = (f32[128,16,2]{0,1,2:T(8,128)}, f32[128,16,2]{0,1,2:T(8,128)}, u32[]{:S(2)}, u32[]{:S(2)}) collective-permute-start(f32[128,16,2]{0,1,2:T(8,128)} %copy.110), channel_id=1, source_target_pairs={{0,16},{1,17},{2,18},{3,19},{4,20},{5,21},{6,22},{7,23},{8,24},{9,... | collective-permute-start | bytes 49160 | tf_op jit(solution)/shard_map/ppermute | solution.py:24
  858.5 8.8 collective-permute-start.25
  911.7 26.7 %collective-permute-start.35 = (f32[128,2,256]{2,1,0:T(2,128)}, f32[128,2,256]{2,1,0:T(2,128)S(1)}, u32[]{:S(2)}, u32[]{:S(2)}) collective-permute-start(f32[128,2,256]{2,1,0:T(2,128)} %get-tuple-element.479), channel_id=1, source_target_pairs={{0,4},{4,8},{8,12},{12,0},{1,5},{5,9},{9,13},{13,1},{2,6},{6,10},{... | collective-permute-start | bytes 786440 | tf_op jit(solution)/shard_map/ppermute | solution.py:24
  911.7 24.9 %collective-permute-start.34 = (f32[128,2,256]{2,1,0:T(2,128)}, f32[128,2,256]{2,1,0:T(2,128)}, u32[]{:S(2)}, u32[]{:S(2)}) collective-permute-start(f32[128,2,256]{2,1,0:T(2,128)} %get-tuple-element.478), channel_id=1, source_target_pairs={{4,0},{8,4},{12,8},{0,12},{5,1},{9,5},{13,9},{1,13},{6,2},{10,6},{... | collective-permute-start | bytes 786440 | tf_op jit(solution)/shard_map/ppermute | solution.py:27
  919.2 12.2 %collective-permute-start.32 = (f32[128,16,2]{0,1,2:T(8,128)}, f32[128,16,2]{0,1,2:T(8,128)S(1)}, u32[]{:S(2)}, u32[]{:S(2)}) collective-permute-start(f32[128,16,2]{0,1,2:T(8,128)} %copy.111), channel_id=1, source_target_pairs={{16,0},{17,1},{18,2},{19,3},{20,4},{21,5},{22,6},{23,7},{24,8},{25... | collective-permute-start | bytes 49160 | tf_op jit(solution)/shard_map/ppermute | solution.py:27
  922.8 11.6 %collective-permute-start.33 = (f32[128,16,2]{0,1,2:T(8,128)}, f32[128,16,2]{0,1,2:T(8,128)}, u32[]{:S(2)}, u32[]{:S(2)}) collective-permute-start(f32[128,16,2]{0,1,2:T(8,128)} %copy.112), channel_id=1, source_target_pairs={{0,16},{1,17},{2,18},{3,19},{4,20},{5,21},{6,22},{7,23},{8,24},{9,... | collective-permute-start | bytes 49160 | tf_op jit(solution)/shard_map/ppermute | solution.py:24
  929.5 8.8 collective-permute-start.31
  931.4 6.9 collective-permute-start.30
  (15 other events, 313.6 us)
where the time goes:
time: 998 us; the launch traced here: 981 us
  other arithmetic  333 us (33%)
  loops' own time  180 us (18%)
  local copies, waits for them, and re-layouts  166 us (17%)
  between operations  126 us (13%)
  blocking collectives  84.3 us (8%)
  starting transfers between devices  81.1 us (8%)
  matrix products  11.7 us (1%)
    another operation x2, loops' own time, local(): lax.linalg.tridiagonal_solve(lower_diag, main_diag, upper_diag, jnp.eye(s...  180 us
    div x6, other arithmetic, settle(): (suf_first - suf_tips[0] * (own_last - own_tips[2] * lower_value)) / (1.0...  80.8 us
    div x5, other arithmetic, local(): lax.linalg.tridiagonal_solve(lower_diag, main_diag, upper_diag, jnp.eye(s...  80.3 us
    add x6, other arithmetic, right_side(): return state_field + spread - transport + mixing  62.1 us
    sub x3, other arithmetic, local(): lax.linalg.tridiagonal_solve(lower_diag, main_diag, upper_diag, jnp.eye(s...  60.5 us
    unnamed x60, local copies, waits for them, and re-layouts  53.3 us
    all_gather x6, blocking collectives, interface(): lax.all_gather(first_row[None], 'rad', axis=0, tiled=True)  45.4 us
    ppermute x18, starting transfers between devices, padded(): lax.ppermute(lax.slice_in_dim(block, block.shape[dim] - width, None, axis...  43.1 us
  transfers between devices with their start and end apart: 36, of which 0 were waited for; matrix products, arithmetic and copies ran while one was open for 33% of the time, Pallas kernels for 0%

commit v1 on v0

v1 whole, which is shorter than its diff:
```python
import functools

import jax
import jax.numpy as jnp
from jax import lax
from jax.experimental import pallas as pl
from jax.experimental.pallas import tpu as pltpu
from jax.sharding import PartitionSpec as P

NR = 512
STEPS = 6
F32 = jnp.float32
MESH = pl.DeviceIdType.MESH
PAD = 8
CH = 32


def join_slabs(left, right):
    head_l, tail_l, tl = left
    head_r, tail_r, tr = right
    divisor = 1.0 - tl[3] * tr[0]
    mid_value = (tail_l - tl[3] * head_r) / divisor
    mid_left = tl[2] / divisor
    mid_right = -tl[3] * tr[1] / divisor
    next_value = head_r - tr[0] * mid_value
    next_left = -tr[0] * mid_left
    next_right = tr[1] - tr[0] * mid_right
    return (
        head_l - tl[1] * next_value,
        tail_r - tr[2] * mid_value,
        (
            tl[0] - tl[1] * next_left,
            -tl[1] * next_right,
            -tr[2] * mid_left,
            tr[3] - tr[2] * mid_right,
        ),
    )


def interface_rows(members, me, n):
    zero = jnp.zeros_like(members[0][0])
    identity = (zero, zero, (zero, zero - 1.0, zero - 1.0, zero))

    def choose(cond, a, b):
        return jax.tree.map(lambda x, y: jnp.where(cond, x, y), a, b)

    prefix = identity
    own = members[0]
    for k in range(n):
        own = choose(k == me, members[k], own)
        prefix = choose(k < me, join_slabs(prefix, members[k]), prefix)
    suffix = identity
    for k in range(n - 1, -1, -1):
        suffix = choose(k > me, join_slabs(members[k], suffix), suffix)
    combined = join_slabs(own, suffix)
    lower = (prefix[1] - prefix[2][3] * combined[0]) / (1.0 - prefix[2][3] * combined[2][0])
    upper = (suffix[0] - suffix[2][0] * (own[1] - own[2][2] * lower)) / (
        1.0 - suffix[2][0] * own[2][3]
    )
    return lower, upper


def kernel(
    n, naz, R, NTL, NZL,
    v, rc, ac, kc, out,
    F, Y, Q, HA, PS, PR, RB0, RBE, RBI, TB, MI, CP, SPK, CF, LU,
    az_ss, az_rs, ax_ss, ax_rs, r0_ss, r0_rs, re_ss, re_rs, ri_ss, ri_rs, t_ss, t_rs,
):
    me = lax.axis_index("rad")
    az = lax.axis_index("az")
    ax = lax.axis_index("ax")
    left = lax.rem(az + naz - 1, naz)
    right = lax.rem(az + 1, naz)
    other = 1 - ax
    peers = [lax.rem(me + d, n) for d in range(1, n)]
    NI = NTL - 4

    barrier = pltpu.get_barrier_semaphore()
    for p in peers:
        pl.semaphore_signal(barrier, inc=1, device_id={"rad": p}, device_id_type=MESH)
    for p in (left, right):
        pl.semaphore_signal(barrier, inc=1, device_id={"az": p}, device_id_type=MESH)
    pl.semaphore_signal(barrier, inc=1, device_id={"ax": other}, device_id_type=MESH)
    pl.semaphore_wait(barrier, n + 2)

    def az_copy(s, side):
        if side == 0:
            src, dst, to = F.at[pl.ds(2, 2), pl.ds(PAD, R)], HA.at[s, 1], left
        else:
            src, dst, to = F.at[pl.ds(NTL, 2), pl.ds(PAD, R)], HA.at[s, 0], right
        return pltpu.make_async_remote_copy(
            src_ref=src, dst_ref=dst, send_sem=az_ss.at[s, side],
            recv_sem=az_rs.at[s, 1 - side], device_id={"az": to}, device_id_type=MESH)

    def ax_copy(s):
        return pltpu.make_async_remote_copy(
            src_ref=PS.at[s], dst_ref=PR.at[s], send_sem=ax_ss.at[s],
            recv_sem=ax_rs.at[s], device_id={"ax": other}, device_id_type=MESH)

    def rad_send(buf, ss, rs, d):
        return pltpu.make_async_remote_copy(
            src_ref=buf.at[me], dst_ref=buf.at[me], send_sem=ss.at[d],
            recv_sem=rs.at[me], device_id={"rad": peers[d]}, device_id_type=MESH)

    def rad_recv(buf, ss, rs, d):
        return pltpu.make_async_remote_copy(
            src_ref=buf.at[me], dst_ref=buf.at[peers[d]], send_sem=ss.at[d],
            recv_sem=rs.at[peers[d]], device_id={"rad": peers[d]}, device_id_type=MESH)

    lane = lax.broadcasted_iota(jnp.int32, (CH, 128), 1)

    def pack(s):
        def body(c, carry):
            r0 = pl.multiple_of(c * CH, CH)

            def one(j, acc):
                edge = jnp.where(
                    ax == 0,
                    F[j + 2, pl.ds(PAD + r0, CH), pl.ds(NZL - 128, 128)],
                    F[j + 2, pl.ds(PAD + r0, CH), pl.ds(0, 128)],
                )
                moved = pltpu.roll(edge, 2 * j + 2 * (1 - ax), 1)
                return jnp.where(lane // 2 == j, moved, acc)

            PS[s, pl.ds(r0, CH), :] = lax.fori_loop(0, NTL, one, jnp.zeros((CH, 128), F32))
            return carry

        lax.fori_loop(0, R // CH, body, 0)

    def fill(j, carry):
        F[j + 2, pl.ds(PAD, R), :] = v[j]
        RB0[me, pl.ds(j, 1), :] = v[j, 0:1, :]
        RB0[me, pl.ds(NTL + j, 1), :] = v[j, R - 1 : R, :]
        return carry

    lax.fori_loop(0, NTL, fill, 0)
    az_copy(0, 0).start()
    az_copy(0, 1).start()
    for d in range(n - 1):
        rad_send(RB0, r0_ss, r0_rs, d).start()
    pack(0)
    ax_copy(0).start()

    lane1 = lax.broadcasted_iota(jnp.int32, (1, 128), 1)

    def forward(i, carry):
        delta, row = carry
        inw = kc[0, pl.ds(i, 1), :]
        outw = kc[1, pl.ds(i, 1), :]
        t = 1.0 + kc[2, pl.ds(i, 1), :] + inw * delta
        inv = 1.0 / (outw + t)
        unit = jnp.where(lane1 == i, 1.0, 0.0)
        row = (unit + inw * row) * inv
        MI[pl.ds(i, 1), :] = row
        CP[pl.ds(i, 1), :] = outw * inv
        return t * inv, row

    lax.fori_loop(0, R, forward, (jnp.ones((1, 128), F32), jnp.zeros((1, 128), F32)))

    def backward(t, row):
        i = R - 2 - t
        row = MI[pl.ds(i, 1), :] + CP[pl.ds(i, 1), :] * row
        MI[pl.ds(i, 1), :] = row
        return row

    lax.fori_loop(0, R - 1, backward, MI[R - 1 : R, :])
    SPK[0] = -kc[0, 0:1, :] * jnp.broadcast_to(MI[:, 0:1], (R, 128))
    SPK[1] = -kc[1, R - 1 : R, :] * jnp.broadcast_to(MI[:, R - 1 : R], (R, 128))
    TB[me, 0:1, :] = SPK[0, 0:1, :]
    TB[me, 1:2, :] = SPK[1, 0:1, :]
    TB[me, 2:3, :] = SPK[0, R - 1 : R, :]
    TB[me, 3:4, :] = SPK[1, R - 1 : R, :]
    TB[me, 4:8, :] = jnp.zeros((4, 128), F32)
    for d in range(n - 1):
        rad_send(TB, t_ss, t_rs, d).start()

    for d in range(n - 1):
        rad_recv(RB0, r0_ss, r0_rs, d).wait_recv()
    below = jnp.maximum(me - 1, 0)
    above = jnp.minimum(me + 1, n - 1)
    LU[0] = jnp.where(me > 0, RB0[below, NTL : 2 * NTL, :], 0.0)
    LU[1] = jnp.where(me < n - 1, RB0[above, 0:NTL, :], 0.0)

    def halo_rows(j, carry):
        F[j + 2, PAD - 1 : PAD, :] = LU[0, pl.ds(j, 1), :]
        F[j + 2, PAD + R : PAD + R + 1, :] = LU[1, pl.ds(j, 1), :]
        return carry

    lax.fori_loop(0, NTL, halo_rows, 0)

    for d in range(n - 1):
        rad_recv(TB, t_ss, t_rs, d).wait_recv()
    members = []
    for k in range(n):
        members.append((
            jnp.where(lane1 == k, 1.0, 0.0),
            jnp.where(lane1 == n + k, 1.0, 0.0),
            tuple(TB[k, q : q + 1, :] for q in range(4)),
        ))
    lower_map, upper_map = interface_rows(members, me, n)
    for m in range(2 * n):
        for h, vec in enumerate((lower_map, upper_map)):
            val = jnp.sum(jnp.where(lane1 == m, vec, 0.0), axis=1, keepdims=True)
            CF[h, m : m + 1, :] = jnp.broadcast_to(val, (1, NZL))

    ml = jnp.where(ax == 1, 1.0, 0.0).astype(F32)
    mr = jnp.where(ax == 0, 1.0, 0.0).astype(F32)

    def wide(x):
        return jnp.concatenate([x] * (NZL // 128), axis=1)

    def solve_one(s, j):
        for c in range(R // CH):
            r0 = c * CH
            rows = pl.ds(PAD + r0, CH)
            f = F[j + 2, rows, :]
            m1, m2 = F[j + 1, rows, :], F[j, rows, :]
            p1, p2 = F[j + 3, rows, :], F[j + 4, rows, :]
            lo = F[j + 2, pl.ds(PAD + r0 - 1, CH), :]
            up = F[j + 2, pl.ds(PAD + r0 + 1, CH), :]
            ct = wide(kc[3, pl.ds(r0, CH), :])
            cl = wide(kc[4, pl.ds(r0, CH), :])
            halo = pltpu.roll(PR[s, pl.ds(r0, CH), :], 128 - 2 * j, 1)
            halo1 = pltpu.roll(halo, 127, 1)
            halo2 = pltpu.roll(halo, 126, 1)
            tiles = [f[:, i * 128 : (i + 1) * 128] for i in range(NZL // 128)]
            shifted = {}
            for k in (1, 2):
                down = [pltpu.roll(t, k, 1) for t in tiles]
                edge = ml * (halo1 if k == 1 else halo)
                shifted[-k] = jnp.concatenate([
                    jnp.where(lane < k, edge if i == 0 else down[i - 1], down[i])
                    for i in range(len(tiles))], axis=1)
                rise = [pltpu.roll(t, 128 - k, 1) for t in tiles]
                edge = mr * (halo1 if k == 1 else halo2)
                shifted[k] = jnp.concatenate([
                    jnp.where(lane >= 128 - k,
                              edge if i == len(tiles) - 1 else rise[i + 1], rise[i])
                    for i in range(len(tiles))], axis=1)
            z1d = shifted[1] - shifted[-1]
            z2d = shifted[2] - shifted[-2]
            z1s = shifted[1] + shifted[-1]
            z2s = shifted[2] + shifted[-2]
            rcv = rc[j, pl.ds(r0, CH), :].astype(F32)
            acv = ac[j, pl.ds(r0, CH), :].astype(F32)
            f30 = 30.0 * f
            q = (
                2.0 * f
                - (0.5 * rcv) * (up - lo)
                - (acv * (1.0 / 12.0)) * (8.0 * z1d - z2d)
                + (0.25 / 12.0) * (16.0 * z1s - z2s - f30)
                + ct * f * (8.0 * (p1 - m1) - (p2 - m2))
                + cl * (16.0 * (p1 + m1) - (p2 + m2) - f30)
            )
            Q[pl.ds(r0, CH), :] = q
        y = jnp.dot(MI[:, 0:R], Q[...], precision=lax.Precision.HIGHEST,
                    preferred_element_type=F32)
        Y[j] = y
        return y[0:1, :], y[R - 1 : R, :]

    def edge_of(e):
        return e + (NTL - 4) * (e // 2)

    def finish(s, j):
        low = LU[0, pl.ds(j, 1), :]
        high = LU[1, pl.ds(j, 1), :]
        for c in range(R // CH):
            rows = pl.ds(PAD + c * CH, CH)
            x = (
                Y[j, pl.ds(c * CH, CH), :]
                - wide(SPK[0, pl.ds(c * CH, CH), :]) * low
                - wide(SPK[1, pl.ds(c * CH, CH), :]) * high
                - F[j + 2, rows, :]
            )
            F[j + 2, rows, :] = x
            out[j, pl.ds(c * CH, CH), :] = x
        F[j + 2, PAD - 1 : PAD, :] = low - F[j + 2, PAD - 1 : PAD, :]
        F[j + 2, PAD + R : PAD + R + 1, :] = high - F[j + 2, PAD + R : PAD + R + 1, :]

    def ends(buf, s, half):
        res = []
        for h in range(2):
            total = None
            for k in range(n):
                for w in range(2):
                    term = (CF[h, w * n + k : w * n + k + 1, :]
                            * buf[s, k, w * half : (w + 1) * half, :])
                    total = term if total is None else total + term
            res.append(total)
        return res

    def step(s, carry):
        ax_copy(s).wait_recv()

        def inner(jj, c):
            first, last = solve_one(s, jj + 2)
            RBI[s, me, pl.ds(jj, 1), :] = first
            RBI[s, me, pl.ds(NI + jj, 1), :] = last
            return c

        lax.fori_loop(0, NI, inner, 0)
        for d in range(n - 1):
            rad_send(RBI.at[s], ri_ss.at[s], ri_rs.at[s], d).start()
        for side in range(2):
            az_copy(s, side).wait_recv()
        for i in range(2):
            F[i, pl.ds(PAD, R), :] = HA[s, 0, i]
            F[NTL + 2 + i, pl.ds(PAD, R), :] = HA[s, 1, i]

        def outer(e, c):
            first, last = solve_one(s, edge_of(e))
            RBE[s, me, pl.ds(e, 1), :] = first
            RBE[s, me, pl.ds(4 + e, 1), :] = last
            return c

        lax.fori_loop(0, 4, outer, 0)
        for d in range(n - 1):
            rad_send(RBE.at[s], re_ss.at[s], re_rs.at[s], d).start()
        for side in range(2):
            az_copy(s, side).wait_send()
        for d in range(n - 1):
            rad_recv(RBE.at[s], re_ss.at[s], re_rs.at[s], d).wait_recv()
        for h, rows in enumerate(ends(RBE, s, 4)):
            LU[h, 0:2, :] = rows[0:2]
            LU[h, NTL - 2 : NTL, :] = rows[2:4]

        def outer2(e, c):
            finish(s, edge_of(e))
            return c

        lax.fori_loop(0, 4, outer2, 0)

        @pl.when(s < STEPS - 1)
        def _():
            az_copy(s + 1, 0).start()
            az_copy(s + 1, 1).start()

        for d in range(n - 1):
            rad_recv(RBI.at[s], ri_ss.at[s], ri_rs.at[s], d).wait_recv()
        for h, rows in enumerate(ends(RBI, s, NI)):
            LU[h, 2 : NTL - 2, :] = rows

        def inner2(jj, c):
            finish(s, jj + 2)
            return c

        lax.fori_loop(0, NI, inner2, 0)

        @pl.when(s < STEPS - 1)
        def _():
            pack(s + 1)
            ax_copy(s + 1).start()

        ax_copy(s).wait_send()
        for d in range(n - 1):
            rad_send(RBE.at[s], re_ss.at[s], re_rs.at[s], d).wait_send()
            rad_send(RBI.at[s], ri_ss.at[s], ri_rs.at[s], d).wait_send()
        return carry

    lax.fori_loop(0, STEPS, step, 0)
    for d in range(n - 1):
        rad_send(RB0, r0_ss, r0_rs, d).wait_send()
        rad_send(TB, t_ss, t_rs, d).wait_send()


def local(n, naz, velocity, radial_courant, axial_courant, radial_diffusion):
    R, NTL, NZL = velocity.shape
    position = (lax.axis_index("rad") * R).astype(F32) + jnp.arange(R).astype(F32)
    spacing = 1.0 / (NR + 1)
    radius = 1.0 + (position + 1.0) * spacing
    inward = radial_diffusion * (radius - 0.5 * spacing) / radius
    outward = radial_diffusion * (radius + 0.5 * spacing) / radius
    sink = radial_diffusion * spacing * spacing / (radius * radius)
    kc = jnp.stack([inward, outward, sink, -(0.25 / 12.0) / radius,
                    (0.25 / 12.0) / (radius * radius)])
    kc = jnp.broadcast_to(kc[:, :, None], (5, R, 128))
    turn = lambda a: jnp.transpose(a, (1, 0, 2))
    S = STEPS
    dma = pltpu.SemaphoreType.DMA
    res = pl.pallas_call(
        functools.partial(kernel, n, naz, R, NTL, NZL),
        out_shape=jax.ShapeDtypeStruct((NTL, R, NZL), F32),
        in_specs=[pl.BlockSpec(memory_space=pltpu.VMEM)] * 4,
        out_specs=pl.BlockSpec(memory_space=pltpu.VMEM),
        scratch_shapes=[
            pltpu.VMEM((NTL + 4, R + 2 * PAD, NZL), F32),
            pltpu.VMEM((NTL, R, NZL), F32),
            pltpu.VMEM((R, NZL), F32),
            pltpu.VMEM((S, 2, 2, R, NZL), F32),
            pltpu.VMEM((S, R, 128), F32),
            pltpu.VMEM((S, R, 128), F32),
            pltpu.VMEM((n, 2 * NTL, NZL), F32),
            pltpu.VMEM((S, n, 8, NZL), F32),
            pltpu.VMEM((S, n, 2 * (NTL - 4), NZL), F32),
            pltpu.VMEM((n, 8, 128), F32),
            pltpu.VMEM((R, 128), F32),
            pltpu.VMEM((R, 128), F32),
            pltpu.VMEM((2, R, 128), F32),
            pltpu.VMEM((2, 2 * n, NZL), F32),
            pltpu.VMEM((2, NTL, NZL), F32),
            dma((S, 2)), dma((S, 2)), dma((S,)), dma((S,)),
            dma((n,)), dma((n,)), dma((S, n)), dma((S, n)),
            dma((S, n)), dma((S, n)), dma((n,)), dma((n,)),
        ],
        compiler_params=pltpu.CompilerParams(
            collective_id=0, has_side_effects=True, vmem_limit_bytes=48 * 1024 * 1024),
    )(turn(velocity), turn(radial_courant), turn(axial_courant), kc)
    return turn(res)


def solution(mesh):
    return jax.shard_map(
        functools.partial(local, mesh.shape["rad"], mesh.shape["az"]),
        mesh=mesh,
        in_specs=(P("rad", "az", "ax"), P("rad", "az", "ax"), P("rad", "az", "ax"), P("rad")),
        out_specs=P("rad", "az", "ax"),
        check_vma=False,
    )
```

time: 998 us -> 141 us (0.14); the launches traced: 981 us -> 141 us
  other arithmetic: 333 us -> 0.68 us
  loops' own time: 180 us -> 0 us
  local copies, waits for them, and re-layouts: 166 us -> 7.71 us
  Pallas kernels: 0 us -> 132 us
  between operations: 126 us -> 0.04 us
  blocking collectives: 84.3 us -> 0 us
  starting transfers between devices: 81.1 us -> 0 us
  matrix products: 11.7 us -> 0 us
    another operation x2 -> x0, loops' own time: 180 us -> none  [local(): lax.linalg.tridiagonal_solve(lower_diag, main_diag, upper_diag, jnp.eye(s...]
    div x11 -> x1, other arithmetic: 161 us -> 0.01 us  [local(): 0.25 / 12.0 / (radius * radius)]
    pallas_call x0 -> x1, Pallas kernels: none -> 132 us  [local(): pl.pallas_call(functools.partial(kernel, n, naz, R, NTL, NZL), out_shape=...]
    ppermute x36 -> x0, starting transfers between devices: 81.1 us -> none  [the longest x18 43.1 us: padded(): lax.ppermute(lax.slice_in_dim(block, block.shape[dim] - width, None, axis...]
    all_gather x12 -> x0, blocking collectives: 78.3 us -> none  [the longest x6 45.4 us: interface(): lax.all_gather(first_row[None], 'rad', axis=0, tiled=True)]
    sub x9 -> x0, other arithmetic: 62.6 us -> none  [the longest x3 60.5 us: local(): lax.linalg.tridiagonal_solve(lower_diag, main_diag, upper_diag, jnp.eye(s...]
    add x7 -> x0, other arithmetic: 62.1 us -> none  [the longest x6 62.1 us: right_side(): return state_field + spread - transport + mixing]
    slice x76 -> x0, local copies, waits for them, and re-layouts: 60.6 us -> none  [the longest x37 23.2 us: local(): lax.linalg.tridiagonal_solve(lower_diag, main_diag, upper_diag, jnp.eye(s...]
  transfers between devices with their start and end apart: 36 -> 0, of which waited for: 0 -> 0; matrix products, arithmetic and copies ran while one was open for 33% -> 0% of each run, Pallas kernels for 0% -> 0%
where the time goes in v1:
time: 141 us
  Pallas kernels  132 us (94%)
  local copies, waits for them, and re-layouts  7.71 us (5%)
    pallas_call x1, Pallas kernels, local(): pl.pallas_call(functools.partial(kernel, n, naz, R, NTL, NZL), out_shape=...  132 us
    unnamed x5, local copies, waits for them, and re-layouts  4.29 us
    transpose x2, local copies, waits for them, and re-layouts, local(): turn = lambda a: jnp.transpose(a, (1, 0, 2))  3.26 us

profile of v1, /device:TPU:0, one launch (start us, length us, event | category | flops | bytes accessed | tf_op | source)
XLA Modules:
  0.0 140.5 jit_solution(2255967466440653298)
XLA Ops:
  0.0 0.7 fusion
  0.7 0.1 broadcast_in_dim.2.kc
  0.9 0.0 copy-start
  0.9 0.0 copy-start.1
  0.9 4.3 %copy.12 = f32[128,16,256]{2,0,1:T(8,128)} copy(f32[128,16,256]{2,1,0:T(8,128)} %param.4) | data formatting | bytes 4194304 | tf_op args[0]
  5.2 0.0 copy-done
  5.2 0.0 copy-done.1
  5.2 0.7 copy_bitcast_fusion.1
  5.9 132.1 %shard_map.46 = f32[16,128,256]{2,1,0:T(8,128)S(1)} custom-call(f32[16,128,256]{2,1,0:T(8,128)} %bitcast.15, bf16[16,128,256]{2,1,0:T(8,128)(2,1)S(1)} %get-tuple-element.11.rc, bf16[16,128,256]{2,1,0:T(8,128)(2,1)S(1)} %get-tuple-element.10.ac, f32[5,128,128]{2,1,0:T(8,128)S(1)} %broadcast_in_dim.2.kc), custom_call_target="tpu_custom_call" | custom-call | tf_op jit(solution)/shard_map/pallas_call | solution.py:380
  138.0 2.5 %copy.8 = f32[128,16,256]{2,1,0:T(8,128)} copy(f32[128,16,256]{2,0,1:T(8,128)S(1)} %bitcast.14) | data formatting | bytes 4194304 | tf_op jit(solution)/shard_map/transpose | solution.py:377
  (2 shorter events, 0.0 us)
Async XLA Ops:
  0.9 4.3 %copy-start = (bf16[128,16,256]{2,1,0:T(8,128)(2,1)S(1)}, bf16[128,16,256]{2,1,0:T(8,128)(2,1)}, u32[]{:S(2)}) copy-start(bf16[128,16,256]{2,1,0:T(8,128)(2,1)} %param.6) | copy-start | bytes 3145732
  0.9 4.3 %copy-start.1 = (bf16[128,16,256]{2,1,0:T(8,128)(2,1)S(1)}, bf16[128,16,256]{2,1,0:T(8,128)(2,1)}, u32[]{:S(2)}) copy-start(bf16[128,16,256]{2,1,0:T(8,128)(2,1)} %param.5) | copy-start | bytes 3145732

commit v2 on v1

--- a/solution.py
+++ b/solution.py
@@ -63,7 +63,7 @@
 def kernel(
     n, naz, R, NTL, NZL,
     v, rc, ac, kc, out,
-    F, Y, Q, HA, PS, PR, RB0, RBE, RBI, TB, MI, CP, SPK, CF, LU,
+    F, Y, Q, RCF, ACF, HA, PS, PR, RB0, RBE, RBI, TB, MA, MB, PHI, PSI, DP, DM, A0, SPK, CF, LU, ST,
     az_ss, az_rs, ax_ss, ax_rs, r0_ss, r0_rs, re_ss, re_rs, ri_ss, ri_rs, t_ss, t_rs,
 ):
     me = lax.axis_index("rad")
@@ -110,30 +110,36 @@
     lane = lax.broadcasted_iota(jnp.int32, (CH, 128), 1)
 
     def pack(s):
+        for c in range(R // CH):
+            rows = pl.ds(PAD + c * CH, CH)
+            acc = jnp.zeros((CH, 128), F32)
+            for j in range(NTL):
+                edge = jnp.where(ax == 0, F[j + 2, rows, pl.ds(NZL - 128, 128)],
+                                 F[j + 2, rows, pl.ds(0, 128)])
+                acc = jnp.where(lane // 2 == j, pltpu.roll(edge, 2 * j + 2 * (1 - ax), 1), acc)
+            PS[s, pl.ds(c * CH, CH), :] = acc
+
+    TILES = NZL // 128
+
+    def stage(ref, scale):
         def body(c, carry):
-            r0 = pl.multiple_of(c * CH, CH)
-
-            def one(j, acc):
-                edge = jnp.where(
-                    ax == 0,
-                    F[j + 2, pl.ds(PAD + r0, CH), pl.ds(NZL - 128, 128)],
-                    F[j + 2, pl.ds(PAD + r0, CH), pl.ds(0, 128)],
-                )
-                moved = pltpu.roll(edge, 2 * j + 2 * (1 - ax), 1)
-                return jnp.where(lane // 2 == j, moved, acc)
-
-            PS[s, pl.ds(r0, CH), :] = lax.fori_loop(0, NTL, one, jnp.zeros((CH, 128), F32))
+            rows = pl.ds(pl.multiple_of(c * 128, 128), 128)
+            for i in range(TILES):
+                x = ref[rows, pl.ds(128 * i, 128)].astype(F32)
+                ST[i, rows, :] = x if scale is None else x * scale
             return carry
 
-        lax.fori_loop(0, R // CH, body, 0)
-
-    def fill(j, carry):
-        F[j + 2, pl.ds(PAD, R), :] = v[j]
-        RB0[me, pl.ds(j, 1), :] = v[j, 0:1, :]
-        RB0[me, pl.ds(NTL + j, 1), :] = v[j, R - 1 : R, :]
-        return carry
-
-    lax.fori_loop(0, NTL, fill, 0)
+        lax.fori_loop(0, R * NTL // 128, body, 0)
+
+    def split_read(i, j):
+        return ST[i, pl.ds(j, R, stride=NTL), :]
+
+    stage(v, None)
+    for j in range(NTL):
+        for i in range(TILES):
+            F[j + 2, pl.ds(PAD, R), pl.ds(128 * i, 128)] = split_read(i, j)
+    RB0[me, 0:NTL, :] = v[0:NTL, :]
+    RB0[me, NTL : 2 * NTL, :] = v[(R - 1) * NTL : R * NTL, :]
     az_copy(0, 0).start()
     az_copy(0, 1).start()
     for d in range(n - 1):
@@ -142,30 +148,33 @@
     ax_copy(0).start()
 
     lane1 = lax.broadcasted_iota(jnp.int32, (1, 128), 1)
-
-    def forward(i, carry):
-        delta, row = carry
-        inw = kc[0, pl.ds(i, 1), :]
-        outw = kc[1, pl.ds(i, 1), :]
-        t = 1.0 + kc[2, pl.ds(i, 1), :] + inw * delta
-        inv = 1.0 / (outw + t)
-        unit = jnp.where(lane1 == i, 1.0, 0.0)
-        row = (unit + inw * row) * inv
-        MI[pl.ds(i, 1), :] = row
-        CP[pl.ds(i, 1), :] = outw * inv
-        return t * inv, row
-
-    lax.fori_loop(0, R, forward, (jnp.ones((1, 128), F32), jnp.zeros((1, 128), F32)))
-
-    def backward(t, row):
-        i = R - 2 - t
-        row = MI[pl.ds(i, 1), :] + CP[pl.ds(i, 1), :] * row
-        MI[pl.ds(i, 1), :] = row
-        return row
-
-    lax.fori_loop(0, R - 1, backward, MI[R - 1 : R, :])
-    SPK[0] = -kc[0, 0:1, :] * jnp.broadcast_to(MI[:, 0:1], (R, 128))
-    SPK[1] = -kc[1, R - 1 : R, :] * jnp.broadcast_to(MI[:, R - 1 : R], (R, 128))
+    ones = jnp.ones((1, 128), F32)
+
+    def march(i, carry):
+        phi, p, psi, m = carry
+        k = R - 1 - i
+        PHI[pl.ds(i, 1), :] = phi
+        PSI[pl.ds(k, 1), :] = psi
+        DM[pl.ds(k, 1), :] = m
+        p = kc[2, pl.ds(i, 1), :] * phi + kc[5, pl.ds(i, 1), :] * p
+        m = kc[6, pl.ds(k, 1), :] * psi + kc[7, pl.ds(k, 1), :] * m
+        DP[pl.ds(i, 1), :] = p
+        return phi + p, p, psi + m, m
+
+    lax.fori_loop(0, R, march, (ones, ones, ones, ones))
+    weight = 1.0 / (kc[1] * (DP[...] * PSI[...] + PHI[...] * DM[...]))
+    at_i = lax.broadcasted_iota(jnp.int32, (R, R), 0)
+    at_j = lax.broadcasted_iota(jnp.int32, (R, R), 1)
+    upper_part = jnp.transpose(PSI[...] * weight)[0:R, :]
+    lower_part = jnp.transpose(PHI[...] * weight)[0:R, :]
+    inverse = jnp.where(at_i <= at_j, PHI[:, 0:R] * upper_part, PSI[:, 0:R] * lower_part)
+    high = inverse.astype(jnp.bfloat16)
+    MA[:, 0:R] = high
+    MA[:, R : 2 * R] = high
+    MB[...] = (inverse - high.astype(F32)).astype(jnp.bfloat16)
+    SPK[0] = -kc[0, 0:1, :] * jnp.broadcast_to(inverse[:, 0:1], (R, 128))
+    SPK[1] = -kc[1, R - 1 : R, :] * jnp.broadcast_to(inverse[:, R - 1 : R], (R, 128))
+    A0[...] = 2.0 - 30.0 * (0.25 / 12.0) - 30.0 * kc[4]
     TB[me, 0:1, :] = SPK[0, 0:1, :]
     TB[me, 1:2, :] = SPK[1, 0:1, :]
     TB[me, 2:3, :] = SPK[0, R - 1 : R, :]
@@ -174,34 +183,36 @@
     for d in range(n - 1):
         rad_send(TB, t_ss, t_rs, d).start()
 
+    for src, dst, scale in ((rc, RCF, -0.5), (ac, ACF, -1.0 / 12.0)):
+        stage(src, scale)
+        for j in range(NTL):
+            for i in range(TILES):
+                dst[j, :, pl.ds(128 * i, 128)] = split_read(i, j)
+
     for d in range(n - 1):
         rad_recv(RB0, r0_ss, r0_rs, d).wait_recv()
     below = jnp.maximum(me - 1, 0)
     above = jnp.minimum(me + 1, n - 1)
-    LU[0] = jnp.where(me > 0, RB0[below, NTL : 2 * NTL, :], 0.0)
-    LU[1] = jnp.where(me < n - 1, RB0[above, 0:NTL, :], 0.0)
-
-    def halo_rows(j, carry):
-        F[j + 2, PAD - 1 : PAD, :] = LU[0, pl.ds(j, 1), :]
-        F[j + 2, PAD + R : PAD + R + 1, :] = LU[1, pl.ds(j, 1), :]
-        return carry
-
-    lax.fori_loop(0, NTL, halo_rows, 0)
+    low0 = jnp.where(me > 0, RB0[below, NTL : 2 * NTL, :], 0.0)
+    high0 = jnp.where(me < n - 1, RB0[above, 0:NTL, :], 0.0)
+    for j in range(NTL):
+        F[j + 2, PAD - 1 : PAD, :] = low0[j : j + 1, :]
+        F[j + 2, PAD + R : PAD + R + 1, :] = high0[j : j + 1, :]
 
     for d in range(n - 1):
         rad_recv(TB, t_ss, t_rs, d).wait_recv()
     members = []
     for k in range(n):
         members.append((
-            jnp.where(lane1 == k, 1.0, 0.0),
-            jnp.where(lane1 == n + k, 1.0, 0.0),
+            jnp.where(lane1 == 2 * k, 1.0, 0.0),
+            jnp.where(lane1 == 2 * k + 1, 1.0, 0.0),
             tuple(TB[k, q : q + 1, :] for q in range(4)),
         ))
     lower_map, upper_map = interface_rows(members, me, n)
     for m in range(2 * n):
         for h, vec in enumerate((lower_map, upper_map)):
             val = jnp.sum(jnp.where(lane1 == m, vec, 0.0), axis=1, keepdims=True)
-            CF[h, m : m + 1, :] = jnp.broadcast_to(val, (1, NZL))
+            CF[h, m // 2, m % 2 : m % 2 + 1, :] = jnp.broadcast_to(val, (1, 128))
 
     ml = jnp.where(ax == 1, 1.0, 0.0).astype(F32)
     mr = jnp.where(ax == 0, 1.0, 0.0).astype(F32)
@@ -241,64 +252,65 @@
             z2d = shifted[2] - shifted[-2]
             z1s = shifted[1] + shifted[-1]
             z2s = shifted[2] + shifted[-2]
-            rcv = rc[j, pl.ds(r0, CH), :].astype(F32)
-            acv = ac[j, pl.ds(r0, CH), :].astype(F32)
-            f30 = 30.0 * f
+            a0 = wide(A0[pl.ds(r0, CH), :])
             q = (
-                2.0 * f
-                - (0.5 * rcv) * (up - lo)
-                - (acv * (1.0 / 12.0)) * (8.0 * z1d - z2d)
-                + (0.25 / 12.0) * (16.0 * z1s - z2s - f30)
-                + ct * f * (8.0 * (p1 - m1) - (p2 - m2))
-                + cl * (16.0 * (p1 + m1) - (p2 + m2) - f30)
+                f * (a0 + ct * (8.0 * (p1 - m1) - (p2 - m2)))
+                + cl * (16.0 * (p1 + m1) - (p2 + m2))
+                + RCF[j, pl.ds(r0, CH), :] * (up - lo)
+                + ACF[j, pl.ds(r0, CH), :] * (8.0 * z1d - z2d)
+                + (0.25 / 12.0) * (16.0 * z1s - z2s)
             )
-            Q[pl.ds(r0, CH), :] = q
-        y = jnp.dot(MI[:, 0:R], Q[...], precision=lax.Precision.HIGHEST,
-                    preferred_element_type=F32)
-        Y[j] = y
-        return y[0:1, :], y[R - 1 : R, :]
+            qh = q.astype(jnp.bfloat16)
+            cols = pl.ds(pl.multiple_of(j * NZL, NZL), NZL)
+            Q[pl.ds(r0, CH), cols] = qh
+            Q[pl.ds(R + r0, CH), cols] = (q - qh.astype(F32)).astype(jnp.bfloat16)
+
+    def multiply(start, width):
+        cols = pl.ds(start, width)
+        y = jnp.dot(MA[...], Q[:, cols], preferred_element_type=F32)
+        Y[:, cols] = y + jnp.dot(MB[...], Q[0:R, cols], preferred_element_type=F32)
 
     def edge_of(e):
         return e + (NTL - 4) * (e // 2)
 
     def finish(s, j):
-        low = LU[0, pl.ds(j, 1), :]
-        high = LU[1, pl.ds(j, 1), :]
+        cols = pl.ds(pl.multiple_of(j * NZL, NZL), NZL)
+        low = LU[0:1, cols]
+        high = LU[1:2, cols]
         for c in range(R // CH):
             rows = pl.ds(PAD + c * CH, CH)
-            x = (
-                Y[j, pl.ds(c * CH, CH), :]
+            F[j + 2, rows, :] = (
+                Y[pl.ds(c * CH, CH), cols]
                 - wide(SPK[0, pl.ds(c * CH, CH), :]) * low
                 - wide(SPK[1, pl.ds(c * CH, CH), :]) * high
                 - F[j + 2, rows, :]
             )
-            F[j + 2, rows, :] = x
-            out[j, pl.ds(c * CH, CH), :] = x
         F[j + 2, PAD - 1 : PAD, :] = low - F[j + 2, PAD - 1 : PAD, :]
         F[j + 2, PAD + R : PAD + R + 1, :] = high - F[j + 2, PAD + R : PAD + R + 1, :]
 
-    def ends(buf, s, half):
+    def ends(buf, s, width):
         res = []
         for h in range(2):
             total = None
             for k in range(n):
-                for w in range(2):
-                    term = (CF[h, w * n + k : w * n + k + 1, :]
-                            * buf[s, k, w * half : (w + 1) * half, :])
-                    total = term if total is None else total + term
-            res.append(total)
+                coef = jnp.concatenate([CF[h, k]] * (width // 128), axis=1)
+                term = coef * buf[s, k]
+                total = term if total is None else total + term
+            res.append(total[0:1, :] + total[1:2, :])
         return res
 
     def step(s, carry):
         ax_copy(s).wait_recv()
 
         def inner(jj, c):
-            first, last = solve_one(s, jj + 2)
-            RBI[s, me, pl.ds(jj, 1), :] = first
-            RBI[s, me, pl.ds(NI + jj, 1), :] = last
+            solve_one(s, jj + 2)
             return c
 
         lax.fori_loop(0, NI, inner, 0)
+        multiply(2 * NZL, NI * NZL)
+        mid = pl.ds(2 * NZL, NI * NZL)
+        RBI[s, me, 0:1, :] = Y[0:1, mid]
+        RBI[s, me, 1:2, :] = Y[R - 1 : R, mid]
         for d in range(n - 1):
             rad_send(RBI.at[s], ri_ss.at[s], ri_rs.at[s], d).start()
         for side in range(2):
@@ -308,21 +320,24 @@
             F[NTL + 2 + i, pl.ds(PAD, R), :] = HA[s, 1, i]
 
         def outer(e, c):
-            first, last = solve_one(s, edge_of(e))
-            RBE[s, me, pl.ds(e, 1), :] = first
-            RBE[s, me, pl.ds(4 + e, 1), :] = last
+            solve_one(s, edge_of(e))
             return c
 
         lax.fori_loop(0, 4, outer, 0)
+        two = 2 * NZL
+        for i, start in enumerate((0, (NTL - 2) * NZL)):
+            multiply(start, two)
+            RBE[s, me, 0:1, i * two : (i + 1) * two] = Y[0:1, start : start + two]
+            RBE[s, me, 1:2, i * two : (i + 1) * two] = Y[R - 1 : R, start : start + two]
         for d in range(n - 1):
             rad_send(RBE.at[s], re_ss.at[s], re_rs.at[s], d).start()
         for side in range(2):
             az_copy(s, side).wait_send()
         for d in range(n - 1):
             rad_recv(RBE.at[s], re_ss.at[s], re_rs.at[s], d).wait_recv()
-        for h, rows in enumerate(ends(RBE, s, 4)):
-            LU[h, 0:2, :] = rows[0:2]
-            LU[h, NTL - 2 : NTL, :] = rows[2:4]
+        for h, row in enumerate(ends(RBE, s, 4 * NZL)):
+            LU[h : h + 1, 0:two] = row[:, 0:two]
+            LU[h : h + 1, (NTL - 2) * NZL : NTL * NZL] = row[:, two : 2 * two]
 
         def outer2(e, c):
             finish(s, edge_of(e))
@@ -337,8 +352,8 @@
 
         for d in range(n - 1):
             rad_recv(RBI.at[s], ri_ss.at[s], ri_rs.at[s], d).wait_recv()
-        for h, rows in enumerate(ends(RBI, s, NI)):
-            LU[h, 2 : NTL - 2, :] = rows
+        for h, row in enumerate(ends(RBI, s, NI * NZL)):
+            LU[h : h + 1, mid] = row
 
         def inner2(jj, c):
             finish(s, jj + 2)
@@ -358,6 +373,17 @@
         return carry
 
     lax.fori_loop(0, STEPS, step, 0)
+    for j in range(NTL):
+        for i in range(NZL // 128):
+            ST[i, pl.ds(j, R, stride=NTL), :] = F[j + 2, pl.ds(PAD, R), pl.ds(128 * i, 128)]
+
+    def unstage(c, carry):
+        rows = pl.ds(pl.multiple_of(c * 128, 128), 128)
+        for i in range(TILES):
+            out[rows, pl.ds(128 * i, 128)] = ST[i, rows, :]
+        return carry
+
+    lax.fori_loop(0, R * NTL // 128, unstage, 0)
     for d in range(n - 1):
         rad_send(RB0, r0_ss, r0_rs, d).wait_send()
         rad_send(TB, t_ss, t_rs, d).wait_send()
@@ -371,41 +397,51 @@
     inward = radial_diffusion * (radius - 0.5 * spacing) / radius
     outward = radial_diffusion * (radius + 0.5 * spacing) / radius
     sink = radial_diffusion * spacing * spacing / (radius * radius)
-    kc = jnp.stack([inward, outward, sink, -(0.25 / 12.0) / radius,
-                    (0.25 / 12.0) / (radius * radius)])
-    kc = jnp.broadcast_to(kc[:, :, None], (5, R, 128))
-    turn = lambda a: jnp.transpose(a, (1, 0, 2))
+    grow = 1.0 + sink
+    kc = jnp.stack([inward, outward, grow / outward, -(0.25 / 12.0) / radius,
+                    (0.25 / 12.0) / (radius * radius), inward / outward,
+                    grow / inward, outward / inward])
+    kc = jnp.broadcast_to(kc[:, :, None], (8, R, 128))
+    flat = lambda a: a.reshape(R * NTL, NZL)
     S = STEPS
     dma = pltpu.SemaphoreType.DMA
     res = pl.pallas_call(
         functools.partial(kernel, n, naz, R, NTL, NZL),
-        out_shape=jax.ShapeDtypeStruct((NTL, R, NZL), F32),
+        out_shape=jax.ShapeDtypeStruct((R * NTL, NZL), F32),
         in_specs=[pl.BlockSpec(memory_space=pltpu.VMEM)] * 4,
         out_specs=pl.BlockSpec(memory_space=pltpu.VMEM),
         scratch_shapes=[
             pltpu.VMEM((NTL + 4, R + 2 * PAD, NZL), F32),
+            pltpu.VMEM((R, NTL * NZL), F32),
+            pltpu.VMEM((2 * R, NTL * NZL), jnp.bfloat16),
             pltpu.VMEM((NTL, R, NZL), F32),
-            pltpu.VMEM((R, NZL), F32),
+            pltpu.VMEM((NTL, R, NZL), F32),
             pltpu.VMEM((S, 2, 2, R, NZL), F32),
             pltpu.VMEM((S, R, 128), F32),
             pltpu.VMEM((S, R, 128), F32),
             pltpu.VMEM((n, 2 * NTL, NZL), F32),
-            pltpu.VMEM((S, n, 8, NZL), F32),
-            pltpu.VMEM((S, n, 2 * (NTL - 4), NZL), F32),
+            pltpu.VMEM((S, n, 2, 4 * NZL), F32),
+            pltpu.VMEM((S, n, 2, (NTL - 4) * NZL), F32),
             pltpu.VMEM((n, 8, 128), F32),
+            pltpu.VMEM((R, 2 * R), jnp.bfloat16),
+            pltpu.VMEM((R, R), jnp.bfloat16),
+            pltpu.VMEM((R, 128), F32),
+            pltpu.VMEM((R, 128), F32),
+            pltpu.VMEM((R, 128), F32),
             pltpu.VMEM((R, 128), F32),
             pltpu.VMEM((R, 128), F32),
             pltpu.VMEM((2, R, 128), F32),
-            pltpu.VMEM((2, 2 * n, NZL), F32),
-            pltpu.VMEM((2, NTL, NZL), F32),
+            pltpu.VMEM((2, n, 2, 128), F32),
+            pltpu.VMEM((2, NTL * NZL), F32),
+            pltpu.VMEM((NZL // 128, R * NTL, 128), F32),
             dma((S, 2)), dma((S, 2)), dma((S,)), dma((S,)),
             dma((n,)), dma((n,)), dma((S, n)), dma((S, n)),
             dma((S, n)), dma((S, n)), dma((n,)), dma((n,)),
         ],
         compiler_params=pltpu.CompilerParams(
             collective_id=0, has_side_effects=True, vmem_limit_bytes=48 * 1024 * 1024),
-    )(turn(velocity), turn(radial_courant), turn(axial_courant), kc)
-    return turn(res)
+    )(flat(velocity), flat(radial_courant), flat(axial_courant), kc)
+    return res.reshape(R, NTL, NZL)
 
 
 def solution(mesh):

time: 141 us -> 125 us (0.89)
  Pallas kernels: 132 us -> 120 us
  local copies, waits for them, and re-layouts: 7.71 us -> 3.99 us
    pallas_call x1, Pallas kernels: 132 us -> 120 us  [local(): pl.pallas_call(functools.partial(kernel, n, naz, R, NTL, NZL), out_shape=...]
    transpose x2 -> x0, local copies, waits for them, and re-layouts: 3.26 us -> none  [local(): turn = lambda a: jnp.transpose(a, (1, 0, 2))]
where the time goes in v2:
time: 125 us
  Pallas kernels  120 us (96%)
  local copies, waits for them, and re-layouts  3.99 us (3%)
  other arithmetic  1.37 us (1%)
    pallas_call x1, Pallas kernels, local(): pl.pallas_call(functools.partial(kernel, n, naz, R, NTL, NZL), out_shape=...  120 us
    unnamed x5, local copies, waits for them, and re-layouts  3.77 us

profile of v2, /device:TPU:0, one launch (start us, length us, event | category | flops | bytes accessed | tf_op | source)
XLA Modules:
  0.0 125.2 jit_solution(9175530906900528315)
XLA Ops:
  0.0 0.7 divide_bitcast_fusion
  0.7 0.7 divide_bitcast_fusion.1
  1.4 0.2 broadcast_in_dim.2.kc
  1.6 0.0 copy-start
  1.6 1.2 copy-done
  2.8 0.0 copy-start.1
  2.8 1.2 copy-done.1
  4.1 119.8 %shard_map.46 = f32[2048,256]{1,0:T(8,128)S(1)} custom-call(f32[2048,256]{1,0:T(8,128)} %bitcast.19, bf16[2048,256]{1,0:T(8,128)(2,1)S(1)} %bitcast.17, bf16[2048,256]{1,0:T(8,128)(2,1)S(1)} %bitcast.18, f32[8,128,128]{2,1,0:T(8,128)S(1)} %broadcast_in_dim.2.kc), custom_call_target="tpu_custom_call" | custom-call | tf_op jit(solution)/shard_map/pallas_call | solution.py:408
  123.8 1.3 %copy.6 = f32[128,16,256]{2,1,0:T(8,128)} copy(f32[128,16,256]{2,1,0:T(8,128)S(1)} %bitcast.16) | data formatting | bytes 4194304
  (3 shorter events, 0.1 us)
Async XLA Ops:
  1.6 1.2 copy-start
  2.8 1.2 copy-start.1

commit v3 on v2

--- a/solution.py
+++ b/solution.py
@@ -63,7 +63,7 @@
 def kernel(
     n, naz, R, NTL, NZL,
     v, rc, ac, kc, out,
-    F, Y, Q, RCF, ACF, HA, PS, PR, RB0, RBE, RBI, TB, MA, MB, PHI, PSI, DP, DM, A0, SPK, CF, LU, ST,
+    F, Y, YE, Q, RCF, ACF, HA, PS, PR, RB0, RBE, RBI, TB, MA, MB, PHI, PSI, DP, DM, A0, SPK, CF, LU, ST,
     az_ss, az_rs, ax_ss, ax_rs, r0_ss, r0_rs, re_ss, re_rs, ri_ss, ri_rs, t_ss, t_rs,
 ):
     me = lax.axis_index("rad")
@@ -83,14 +83,12 @@
     pl.semaphore_signal(barrier, inc=1, device_id={"ax": other}, device_id_type=MESH)
     pl.semaphore_wait(barrier, n + 2)
 
-    def az_copy(s, side):
-        if side == 0:
-            src, dst, to = F.at[pl.ds(2, 2), pl.ds(PAD, R)], HA.at[s, 1], left
-        else:
-            src, dst, to = F.at[pl.ds(NTL, 2), pl.ds(PAD, R)], HA.at[s, 0], right
+    def az_copy(s, half, side):
+        first, to = ((2, left), (NTL, right))[side]
         return pltpu.make_async_remote_copy(
-            src_ref=src, dst_ref=dst, send_sem=az_ss.at[s, side],
-            recv_sem=az_rs.at[s, 1 - side], device_id={"az": to}, device_id_type=MESH)
+            src_ref=F.at[pl.ds(first, 2), pl.ds(PAD, R), pl.ds(128 * half, 128)],
+            dst_ref=HA.at[s, half, 1 - side], send_sem=az_ss.at[s, half, side],
+            recv_sem=az_rs.at[s, half, 1 - side], device_id={"az": to}, device_id_type=MESH)
 
     def ax_copy(s):
         return pltpu.make_async_remote_copy(
@@ -140,8 +138,9 @@
             F[j + 2, pl.ds(PAD, R), pl.ds(128 * i, 128)] = split_read(i, j)
     RB0[me, 0:NTL, :] = v[0:NTL, :]
     RB0[me, NTL : 2 * NTL, :] = v[(R - 1) * NTL : R * NTL, :]
-    az_copy(0, 0).start()
-    az_copy(0, 1).start()
+    for half in range(NZL // 128):
+        az_copy(0, half, 0).start()
+        az_copy(0, half, 1).start()
     for d in range(n - 1):
         rad_send(RB0, r0_ss, r0_rs, d).start()
     pack(0)
@@ -220,13 +219,11 @@
     def wide(x):
         return jnp.concatenate([x] * (NZL // 128), axis=1)
 
-    def solve_one(s, j):
+    def solve_one(s, j, inner):
         for c in range(R // CH):
             r0 = c * CH
             rows = pl.ds(PAD + r0, CH)
             f = F[j + 2, rows, :]
-            m1, m2 = F[j + 1, rows, :], F[j, rows, :]
-            p1, p2 = F[j + 3, rows, :], F[j + 4, rows, :]
             lo = F[j + 2, pl.ds(PAD + r0 - 1, CH), :]
             up = F[j + 2, pl.ds(PAD + r0 + 1, CH), :]
             ct = wide(kc[3, pl.ds(r0, CH), :])
@@ -254,16 +251,55 @@
             z2s = shifted[2] + shifted[-2]
             a0 = wide(A0[pl.ds(r0, CH), :])
             q = (
-                f * (a0 + ct * (8.0 * (p1 - m1) - (p2 - m2)))
-                + cl * (16.0 * (p1 + m1) - (p2 + m2))
+                f * a0
                 + RCF[j, pl.ds(r0, CH), :] * (up - lo)
                 + ACF[j, pl.ds(r0, CH), :] * (8.0 * z1d - z2d)
                 + (0.25 / 12.0) * (16.0 * z1s - z2s)
             )
+            cols = pl.ds(pl.multiple_of(j * NZL, NZL), NZL)
+            if not inner:
+                Y[pl.ds(r0, CH), cols] = q
+                continue
+            m1, m2 = F[j + 1, rows, :], F[j, rows, :]
+            p1, p2 = F[j + 3, rows, :], F[j + 4, rows, :]
+            q = q + f * (ct * (8.0 * (p1 - m1) - (p2 - m2)))
+            q = q + cl * (16.0 * (p1 + m1) - (p2 + m2))
             qh = q.astype(jnp.bfloat16)
-            cols = pl.ds(pl.multiple_of(j * NZL, NZL), NZL)
             Q[pl.ds(r0, CH), cols] = qh
             Q[pl.ds(R + r0, CH), cols] = (q - qh.astype(F32)).astype(jnp.bfloat16)
+
+    def edge_terms(half, e):
+        j = edge_of(e)
+        lanes = pl.ds(128 * half, 128)
+        cols = pl.ds(pl.multiple_of(j * NZL + 128 * half, 128), 128)
+        packed = pl.ds(pl.multiple_of(e * 128, 128), 128)
+        for c in range(R // CH):
+            r0 = c * CH
+            rows = pl.ds(PAD + r0, CH)
+            f = F[j + 2, rows, lanes]
+            m1, m2 = F[j + 1, rows, lanes], F[j, rows, lanes]
+            p1, p2 = F[j + 3, rows, lanes], F[j + 4, rows, lanes]
+            q = (
+                Y[pl.ds(r0, CH), cols]
+                + f * (kc[3, pl.ds(r0, CH), :] * (8.0 * (p1 - m1) - (p2 - m2)))
+                + kc[4, pl.ds(r0, CH), :] * (16.0 * (p1 + m1) - (p2 + m2))
+            )
+            qh = q.astype(jnp.bfloat16)
+            Q[pl.ds(r0, CH), packed] = qh
+            Q[pl.ds(R + r0, CH), packed] = (q - qh.astype(F32)).astype(jnp.bfloat16)
+
+    def edge_finish(half, e, low, high):
+        j = edge_of(e)
+        lanes = pl.ds(128 * half, 128)
+        for c in range(R // CH):
+            rows = pl.ds(PAD + c * CH, CH)
+            here = pl.ds(c * CH, CH)
+            F[j + 2, rows, lanes] = (
+                YE[here, pl.ds(e * 128, 128)] - SPK[0, here, :] * low
+                - SPK[1, here, :] * high - F[j + 2, rows, lanes]
+            )
+        F[j + 2, PAD - 1 : PAD, lanes] = low - F[j + 2, PAD - 1 : PAD, lanes]
+        F[j + 2, PAD + R : PAD + R + 1, lanes] = high - F[j + 2, PAD + R : PAD + R + 1, lanes]
 
     def multiply(start, width):
         cols = pl.ds(start, width)
@@ -294,7 +330,7 @@
             total = None
             for k in range(n):
                 coef = jnp.concatenate([CF[h, k]] * (width // 128), axis=1)
-                term = coef * buf[s, k]
+                term = coef * buf[(*s, k)]
                 total = term if total is None else total + term
             res.append(total[0:1, :] + total[1:2, :])
         return res
@@ -303,7 +339,7 @@
         ax_copy(s).wait_recv()
 
         def inner(jj, c):
-            solve_one(s, jj + 2)
+            solve_one(s, jj + 2, True)
             return c
 
         lax.fori_loop(0, NI, inner, 0)
@@ -313,46 +349,45 @@
         RBI[s, me, 1:2, :] = Y[R - 1 : R, mid]
         for d in range(n - 1):
             rad_send(RBI.at[s], ri_ss.at[s], ri_rs.at[s], d).start()
-        for side in range(2):
-            az_copy(s, side).wait_recv()
-        for i in range(2):
-            F[i, pl.ds(PAD, R), :] = HA[s, 0, i]
-            F[NTL + 2 + i, pl.ds(PAD, R), :] = HA[s, 1, i]
-
         def outer(e, c):
-            solve_one(s, edge_of(e))
+            solve_one(s, edge_of(e), False)
             return c
 
         lax.fori_loop(0, 4, outer, 0)
-        two = 2 * NZL
-        for i, start in enumerate((0, (NTL - 2) * NZL)):
-            multiply(start, two)
-            RBE[s, me, 0:1, i * two : (i + 1) * two] = Y[0:1, start : start + two]
-            RBE[s, me, 1:2, i * two : (i + 1) * two] = Y[R - 1 : R, start : start + two]
-        for d in range(n - 1):
-            rad_send(RBE.at[s], re_ss.at[s], re_rs.at[s], d).start()
-        for side in range(2):
-            az_copy(s, side).wait_send()
-        for d in range(n - 1):
-            rad_recv(RBE.at[s], re_ss.at[s], re_rs.at[s], d).wait_recv()
-        for h, row in enumerate(ends(RBE, s, 4 * NZL)):
-            LU[h : h + 1, 0:two] = row[:, 0:two]
-            LU[h : h + 1, (NTL - 2) * NZL : NTL * NZL] = row[:, two : 2 * two]
-
-        def outer2(e, c):
-            finish(s, edge_of(e))
-            return c
-
-        lax.fori_loop(0, 4, outer2, 0)
-
-        @pl.when(s < STEPS - 1)
-        def _():
-            az_copy(s + 1, 0).start()
-            az_copy(s + 1, 1).start()
+        for half in range(NZL // 128):
+            lanes = pl.ds(128 * half, 128)
+            for side in range(2):
+                az_copy(s, half, side).wait_recv()
+            for i in range(2):
+                F[i, pl.ds(PAD, R), lanes] = HA[s, half, 0, i]
+                F[NTL + 2 + i, pl.ds(PAD, R), lanes] = HA[s, half, 1, i]
+            for e in range(4):
+                edge_terms(half, e)
+            y = jnp.dot(MA[...], Q[:, 0:512], preferred_element_type=F32)
+            y = y + jnp.dot(MB[...], Q[0:R, 0:512], preferred_element_type=F32)
+            YE[...] = y
+            RBE[s, half, me, 0:1, :] = y[0:1, :]
+            RBE[s, half, me, 1:2, :] = y[R - 1 : R, :]
+            buf, ss, rs = RBE.at[s, half], re_ss.at[s, half], re_rs.at[s, half]
+            for d in range(n - 1):
+                rad_send(buf, ss, rs, d).start()
+            for side in range(2):
+                az_copy(s, half, side).wait_send()
+            for d in range(n - 1):
+                rad_recv(buf, ss, rs, d).wait_recv()
+            low, high = ends(RBE, (s, half), 512)
+            for e in range(4):
+                edge_finish(half, e, low[:, e * 128 : (e + 1) * 128],
+                            high[:, e * 128 : (e + 1) * 128])
+
+            @pl.when(s < STEPS - 1)
+            def _():
+                az_copy(s + 1, half, 0).start()
+                az_copy(s + 1, half, 1).start()
 
         for d in range(n - 1):
             rad_recv(RBI.at[s], ri_ss.at[s], ri_rs.at[s], d).wait_recv()
-        for h, row in enumerate(ends(RBI, s, NI * NZL)):
+        for h, row in enumerate(ends(RBI, (s,), NI * NZL)):
             LU[h : h + 1, mid] = row
 
         def inner2(jj, c):
@@ -368,7 +403,8 @@
 
         ax_copy(s).wait_send()
         for d in range(n - 1):
-            rad_send(RBE.at[s], re_ss.at[s], re_rs.at[s], d).wait_send()
+            for half in range(NZL // 128):
+                rad_send(RBE.at[s, half], re_ss.at[s, half], re_rs.at[s, half], d).wait_send()
             rad_send(RBI.at[s], ri_ss.at[s], ri_rs.at[s], d).wait_send()
         return carry
 
@@ -413,14 +449,15 @@
         scratch_shapes=[
             pltpu.VMEM((NTL + 4, R + 2 * PAD, NZL), F32),
             pltpu.VMEM((R, NTL * NZL), F32),
+            pltpu.VMEM((R, 512), F32),
             pltpu.VMEM((2 * R, NTL * NZL), jnp.bfloat16),
             pltpu.VMEM((NTL, R, NZL), F32),
             pltpu.VMEM((NTL, R, NZL), F32),
-            pltpu.VMEM((S, 2, 2, R, NZL), F32),
+            pltpu.VMEM((S, NZL // 128, 2, 2, R, 128), F32),
             pltpu.VMEM((S, R, 128), F32),
             pltpu.VMEM((S, R, 128), F32),
             pltpu.VMEM((n, 2 * NTL, NZL), F32),
-            pltpu.VMEM((S, n, 2, 4 * NZL), F32),
+            pltpu.VMEM((S, NZL // 128, n, 2, 512), F32),
             pltpu.VMEM((S, n, 2, (NTL - 4) * NZL), F32),
             pltpu.VMEM((n, 8, 128), F32),
             pltpu.VMEM((R, 2 * R), jnp.bfloat16),
@@ -434,8 +471,8 @@
             pltpu.VMEM((2, n, 2, 128), F32),
             pltpu.VMEM((2, NTL * NZL), F32),
             pltpu.VMEM((NZL // 128, R * NTL, 128), F32),
-            dma((S, 2)), dma((S, 2)), dma((S,)), dma((S,)),
-            dma((n,)), dma((n,)), dma((S, n)), dma((S, n)),
+            dma((S, NZL // 128, 2)), dma((S, NZL // 128, 2)), dma((S,)), dma((S,)),
+            dma((n,)), dma((n,)), dma((S, NZL // 128, n)), dma((S, NZL // 128, n)),
             dma((S, n)), dma((S, n)), dma((n,)), dma((n,)),
         ],
         compiler_params=pltpu.CompilerParams(

time: 125 us -> 124 us (level)
  Pallas kernels: 120 us -> 118 us
    pallas_call x1, Pallas kernels: 120 us -> 118 us  [local(): pl.pallas_call(functools.partial(kernel, n, naz, R, NTL, NZL), out_shape=...]
where the time goes in v3:
time: 124 us; the launch traced here: 123 us
  Pallas kernels  118 us (95%)
  local copies, waits for them, and re-layouts  3.99 us (3%)
  other arithmetic  1.37 us (1%)
    pallas_call x1, Pallas kernels, local(): pl.pallas_call(functools.partial(kernel, n, naz, R, NTL, NZL), out_shape=...  118 us
    unnamed x5, local copies, waits for them, and re-layouts  3.77 us

profile of v3, /device:TPU:0, one launch (start us, length us, event | category | flops | bytes accessed | tf_op | source)
XLA Modules:
  0.0 123.5 jit_solution(6755201987859003787)
XLA Ops:
  0.0 0.7 divide_bitcast_fusion
  0.7 0.7 divide_bitcast_fusion.1
  1.4 0.2 broadcast_in_dim.2.kc
  1.6 0.0 copy-start
  1.6 1.2 copy-done
  2.8 0.0 copy-start.1
  2.8 1.2 copy-done.1
  4.1 118.1 %shard_map.46 = f32[2048,256]{1,0:T(8,128)S(1)} custom-call(f32[2048,256]{1,0:T(8,128)} %bitcast.19, bf16[2048,256]{1,0:T(8,128)(2,1)S(1)} %bitcast.17, bf16[2048,256]{1,0:T(8,128)(2,1)S(1)} %bitcast.18, f32[8,128,128]{2,1,0:T(8,128)S(1)} %broadcast_in_dim.2.kc), custom_call_target="tpu_custom_call" | custom-call | tf_op jit(solution)/shard_map/pallas_call | solution.py:444
  122.1 1.3 %copy.6 = f32[128,16,256]{2,1,0:T(8,128)} copy(f32[128,16,256]{2,1,0:T(8,128)S(1)} %bitcast.16) | data formatting | bytes 4194304
  (3 shorter events, 0.1 us)
Async XLA Ops:
  1.6 1.2 copy-start
  2.8 1.2 copy-start.1
